TPU v7x, 512 devices: a whole 4x4x16 slice. The times are simulated.
512 devices in a mesh: row: 16 (over x_hi, y, core), col: 32 (over x_lo, z).
Axes of the slice: x: 4 (x_hi: 2, x_lo: 2; x = x_hi * 2 + x_lo), y: 4, z: 16, core: 2. Of those that a mesh axis runs over, the one named last changes fastest.
Arguments:
- grads: bfloat16 [4096, 8192], P('row', 'col'), may hold values from -64 to 64
Outputs:
- kernel: float32 [4096, 4096], P('row', 'col')
All inputs are finite; a program needn't handle non-finite values.
Results may differ from a plain program's by a relative error of at most 0.002.
Values may be sent and summed in bfloat16 or wider, within the bound.
A program may use at most 64 MiB of HBM per device.

v0:
```python
import jax
import jax.numpy as jnp
from jax import lax
from jax.sharding import PartitionSpec as P

K = 8192
BW = 64


def spread(block, axis, owner):
    block = jnp.where(lax.axis_index(axis) == owner, block, jnp.zeros_like(block))
    return lax.psum(block, axis)


def blocked(rows_in):
    count = rows_in.shape[0]
    step = min(count, 128)
    return rows_in.reshape(count // step, step, rows_in.shape[1] // BW, BW)


def layer_fisher(rows_in):
    values = rows_in.reshape(rows_in.shape[0], rows_in.shape[1] // BW, BW)
    return jnp.einsum("nlb,nlc->lbc", values, values, preferred_element_type=jnp.float32)


def factor(total, count):
    width = total.shape[-1]
    unit = jnp.eye(width, dtype=jnp.float32)
    fisher = total / count + 0.1 * unit
    lower = jnp.linalg.cholesky(fisher)
    return jax.vmap(lambda matrix: jax.scipy.linalg.solve_triangular(matrix, unit, lower=True))(
        lower
    )


def whiten(rows_in, inverse):

    def apply_block(block):
        values = block.astype(jnp.float32)
        return jnp.einsum("nlb,lcb->nlc", values, inverse, precision=lax.Precision.HIGHEST).astype(
            jnp.bfloat16
        )

    return lax.map(apply_block, blocked(rows_in)).reshape(rows_in.shape)


def per_device(grads):
    count = grads.shape[0]
    total_count = count * lax.axis_size("row")
    total = lax.psum(layer_fisher(grads), "row")
    features = lax.all_gather(whiten(grads, factor(total, total_count)), "col", axis=1, tiled=True)
    block = count // 2
    column = lax.axis_index("col")
    mine = lax.dynamic_slice_in_dim(features, column % 2 * block, block, 0)
    partner = spread(mine, "row", column // 2)
    scale = K ** (-0.5)

    def product(half):
        left = features[half * block : (half + 1) * block]
        return (
            lax.dot_general(
                left, partner, (((1,), (1,)), ((), ())), preferred_element_type=jnp.float32
            )
            * scale
        )

    return jnp.concatenate([product(0), product(1)], axis=0)


def solution(mesh):
    in_specs = (P("row", "col"),)
    out_specs = P("row", "col")
    return jax.shard_map(
        per_device, mesh=mesh, in_specs=in_specs, out_specs=out_specs, check_vma=False
    )
```

profile of v0, /device:TPU:1, one launch (start us, length us, event | category | flops | bytes accessed | tf_op | source)
XLA Modules:
  0.0 522.4 jit_solution(5046134331172500435)
XLA Ops:
  6.5 0.0 all-reduce.3.cloned.1.call-start
  6.5 1.0 copy.17
  7.5 0.8 fusion.21
  8.4 0.0 all-reduce.3.cloned.1.call-update
  8.4 0.0 all-gather.2.cloned.1.call-start
  8.5 1.1 reshape.31
  9.6 0.1 copy.19
  9.7 0.2 copy.22
  9.9 157.6 %all-reduce.3.cloned.1.call-done = f32[4,64,64]{1,2,0:T(8,128)} async-done(((f32[4,64,64]{1,2,0:T(8,128)}), f32[4,64,64]{1,2,0:T(8,128)}) %all-reduce.3.cloned.1.call-update) | async-done | bytes 65552 | tf_op jit(solution)/shard_map/psum | solution.py:50
  167.5 0.9 multiply_add_fusion
  168.4 0.1 copy.20
  168.5 0.9 fusion.17
  169.5 23.5 %custom-call.8 = f32[4,64,64]{2,1,0:T(8,128)S(1)} custom-call(f32[4,64,64]{2,1,0:T(8,128)S(1)} %fusion.17), custom_call_target="Cholesky" | custom-call | tf_op jit(solution)/shard_map/jit(cholesky)/cholesky | solution.py:30
  192.9 0.1 compare_reduce_fusion
  193.1 0.1 select_bitcast_fusion
  193.2 19.7 %custom-call.9 = f32[4,1,64,64]{2,3,1,0:T(8,128)S(1)} custom-call(f32[4,1,64,64]{3,2,1,0:T(8,128)S(1)} %select_bitcast_fusion), custom_call_target="InvertDiagBlocksLowerTriangular" | custom-call | tf_op jit(solution)/shard_map/vmap(jit(_solve_triangular))/triangular_solve | solution.py:31
  212.8 0.4 fusion.15
  213.2 0.5 while.10
  213.2 0.2 fusion.32
  213.5 0.2 fusion.32
  213.7 0.1 copy.23
  213.9 0.7 copy.30
  214.5 0.0 all-gather.2.cloned.1.call-update
  214.6 0.0 all-reduce.5.cloned.1.call-start
  214.6 121.8 %all-gather.2.cloned.1.call-done = bf16[256,8192]{0,1:T(8,128)(2,1)} async-done(((bf16[256,256]{0,1:T(8,128)(2,1)}), bf16[256,8192]{0,1:T(8,128)(2,1)}) %all-gather.2.cloned.1.call-update) | async-done | bytes 4194320 | tf_op jit(solution)/shard_map/all_gather | solution.py:51
  336.5 3.3 dynamic-slice_select_fusion
  339.8 0.0 all-reduce.5.cloned.1.call-update
  339.8 169.5 %all-reduce.5.cloned.1.call-done = bf16[128,8192]{0,1:T(8,128)(2,1)} async-done(((bf16[128,8192]{0,1:T(8,128)(2,1)}), bf16[128,8192]{0,1:T(8,128)(2,1)}) %all-reduce.5.cloned.1.call-update) | async-done | bytes 2097168 | tf_op jit(solution)/shard_map/psum | solution.py:12
  509.3 0.0 copy-start
  509.3 3.1 fusion.12
  512.5 0.3 copy-done
  512.8 2.4 fusion.9
  515.2 0.7 pad_maximum_fusion
  (6 shorter events, 0.1 us)
Async XLA Ops:
  6.5 161.0 %all-reduce.3.cloned.1.call-start = ((), (), s32[]{:S(2)}) async-start(), calls=%async_computation | async-start | bytes 262144 | tf_op jit(solution)/shard_map/psum | solution.py:50
  8.4 328.1 %all-gather.2.cloned.1.call-start = ((), (), s32[]{:S(2)}) async-start(), calls=%async_computation.1 | async-start | bytes 4325376 | tf_op jit(solution)/shard_map/all_gather | solution.py:51
  214.6 294.8 %all-reduce.5.cloned.1.call-start = ((), (), s32[]{:S(2)}) async-start(), calls=%async_computation.2 | async-start | bytes 4194304 | tf_op jit(solution)/shard_map/psum | solution.py:12
  509.3 3.4 copy-start
Sparse Core Ops, SparseCore 0:
  10.3 157.2 all-reduce.2
  214.7 121.7 all-gather.1
  340.0 169.3 all-reduce.4
where the time goes:
time: 523 us; the launch traced here: 522 us
  waiting for transfers between devices  449 us (86%)
  other arithmetic  49.2 us (9%)
  between operations  13.2 us (3%)
  matrix products  7.15 us (1%)
    psum x1, waiting for transfers between devices, spread(): return lax.psum(block, axis)  170 us
    psum x1, waiting for transfers between devices, per_device(): total = lax.psum(layer_fisher(grads), 'row')  158 us
    all_gather x1, waiting for transfers between devices, per_device(): lax.all_gather(whiten(grads, factor(total, total_count)), 'col', axis=1,...  122 us
    another operation x4, other arithmetic, factor(): lower = jnp.linalg.cholesky(fisher)  23.6 us
    another operation x3, other arithmetic, factor(): jax.scipy.linalg.solve_triangular(matrix, unit, lower=True)  19.8 us
  transfers between devices with their start and end apart: 3, of which 3 were waited for; matrix products, arithmetic and copies ran while one was open for 0% of the time, Pallas kernels for 0%

commit v1 on v0

v1 whole, which is shorter than its diff:
```python
import functools

import jax
import jax.numpy as jnp
from jax import lax
from jax.experimental import pallas as pl
from jax.experimental.pallas import tpu as pltpu
from jax.sharding import PartitionSpec as P

BW = 64
F32 = jnp.float32
BF16 = jnp.bfloat16
MESH = pl.DeviceIdType.MESH
NT = (((1,), (1,)), ((), ()))
TN = (((0,), (0,)), ((), ()))


def eliminate(blocks, inverse, start):
    lane = lax.broadcasted_iota(jnp.int32, (1, 1, 8, 128), 3)
    sub = lax.broadcasted_iota(jnp.int32, (1, 1, 8, 128), 2)
    place = lax.broadcasted_iota(jnp.int32, (8, 1, 8, 128), 0)
    low = lane < BW
    for j in range(8):
        row = blocks[0:1, :, j : j + 1, :]
        other = inverse[0:1, :, j : j + 1, :]
        column = jnp.where(low, blocks[:, :, :, j : j + 1], blocks[:, :, :, BW + j : BW + j + 1])
        pivot = jnp.where(low[:, :, 0:1], row[:, :, :, j : j + 1], row[:, :, :, BW + j : BW + j + 1])
        below = ((place == 0) & (sub > j)) | ((place > 0) & (place + start < 8))
        factor = jnp.where(below, column / pivot, 0.0)
        blocks = blocks - factor * row
        inverse = inverse - factor * other
        scale = jnp.where((place == 0) & (sub == j), lax.rsqrt(pivot), 1.0)
        inverse = inverse * scale
    return blocks, inverse


def rotate(blocks):
    return jnp.concatenate([blocks[1:], blocks[:1]], axis=0)


def kernel(
    n,
    g_ref,
    out_ref,
    rows,
    cols,
    fsend,
    frecv,
    full,
    linv,
    inv,
    part,
    precv,
    ring_send,
    ring_recv,
    col_send,
    col_recv,
    colg_send,
    colg_recv,
    colx_send,
    colx_recv,
    rs_send,
    rs_recv,
    ag_send,
    ag_recv,
    ze_send,
    ze_recv,
    ig_send,
    ig_recv,
    ix_send,
    ix_recv,
    p_send,
    p_recv,
):
    r = lax.axis_index("row")
    c = lax.axis_index("col")
    half = n // 2
    x_lo = c // n
    z = lax.rem(c, n)
    x_hi = r // half
    pair = r // 2
    core = lax.rem(r, 2)
    base = x_lo * n
    depth = 128 // n

    def at(row, plane):
        return {"row": row, "col": base + plane}

    barrier = pltpu.get_barrier_semaphore()

    def greet(d, _):
        pl.semaphore_signal(barrier, 1, device_id=at(lax.rem(r + d, n), z), device_id_type=MESH)
        pl.semaphore_signal(barrier, 1, device_id=at(r, lax.rem(z + d, n)), device_id_type=MESH)
        return 0

    lax.fori_loop(1, n, greet, 0)
    pl.semaphore_signal(
        barrier, 1, device_id={"row": r, "col": (1 - x_lo) * n + z}, device_id_type=MESH
    )
    for k in range(2):
        source = k * half + z // 2
        away = (source != r) | (r != z)

        @pl.when(away)
        def _(source=source):
            pl.semaphore_signal(barrier, 1, device_id=at(source, r), device_id_type=MESH)

    elsewhere = 0
    for h in range(2):
        target = 2 * lax.rem(r, half) + h
        elsewhere += jnp.where((target != z) | (r != z), 1, 0)
    pl.semaphore_wait(barrier, 2 * (n - 1) + 1 + elsewhere)

    right = lax.rem(z + 1, n)
    left = lax.rem(z + n - 1, n)

    def send(source, slot, chunk, plane):
        pltpu.make_async_remote_copy(
            src_ref=source,
            dst_ref=rows.at[slot, chunk],
            send_sem=ring_send,
            recv_sem=ring_recv.at[slot, chunk],
            device_id=at(r, plane),
            device_id_type=MESH,
        ).start()

    def arrived(slot, chunk):
        pltpu.make_async_copy(
            rows.at[slot, chunk], rows.at[slot, chunk], ring_recv.at[slot, chunk]
        ).wait()

    def ring_step(t):
        back = lax.rem(z - t + n, n)
        ahead = lax.rem(z + t, n)
        for slot, chunk, plane in (
            (back, 0, right),
            (ahead, 1, left),
            (back, 1, right),
            (ahead, 0, left),
        ):
            if t == half - 1 and chunk != (0 if plane is right else 1):
                if t > 0:
                    arrived(slot, chunk)
                continue
            if t == 0:
                send(g_ref.at[pl.ds(chunk * 128, 128)], slot, chunk, plane)
            else:
                arrived(slot, chunk)
                send(rows.at[slot, chunk], slot, chunk, plane)

    ring_step(0)

    for h in range(2):
        target = 2 * lax.rem(r, half) + h
        mine = (target == z) & (r == z)
        spot = cols.at[z // 2, lax.rem(z, 2), x_hi]

        @pl.when(mine)
        def _(h=h, spot=spot):
            pltpu.make_async_copy(g_ref.at[pl.ds(h * 128, 128)], spot, col_recv).start()

        @pl.when(jnp.logical_not(mine))
        def _(h=h, spot=spot, target=target):
            pltpu.make_async_remote_copy(
                src_ref=g_ref.at[pl.ds(h * 128, 128)],
                dst_ref=spot,
                send_sem=col_send.at[h],
                recv_sem=col_recv,
                device_id=at(z, target),
                device_id_type=MESH,
            ).start()

    gram = lax.dot_general(g_ref[...], g_ref[...], TN, preferred_element_type=F32)
    lane = lax.broadcasted_iota(jnp.int32, (BW, 128), 1)
    packed = jnp.concatenate(
        [
            jnp.where(
                lane < BW,
                gram[128 * m : 128 * m + BW, 128 * m : 128 * m + 128],
                gram[128 * m + BW : 128 * m + 128, 128 * m : 128 * m + 128],
            )
            for m in range(2)
        ],
        axis=0,
    )
    fsend[...] = packed.reshape(n, depth, 128)

    def scatter(d, _):
        to = lax.rem(r + d, n)
        pltpu.make_async_remote_copy(
            src_ref=fsend.at[to],
            dst_ref=frecv.at[r],
            send_sem=rs_send,
            recv_sem=rs_recv,
            device_id=at(to, z),
            device_id_type=MESH,
        ).start()
        return 0

    lax.fori_loop(1, n, scatter, 0)
    frecv[r] = fsend[r]
    rows[z] = g_ref[...].reshape(2, 128, 256)

    def drain(ref, sem):
        pltpu.make_async_copy(ref, ref, sem).wait()

    drain(frecv.at[pl.ds(0, n - 1)], rs_recv)
    total = frecv[0]
    for i in range(1, n):
        total = total + frecv[i]
    full[r] = total

    def share(d, _):
        pltpu.make_async_remote_copy(
            src_ref=full.at[r],
            dst_ref=full.at[r],
            send_sem=ag_send,
            recv_sem=ag_recv,
            device_id=at(lax.rem(r + d, n), z),
            device_id_type=MESH,
        ).start()
        return 0

    lax.fori_loop(1, n, share, 0)

    def maybe_ring(t):
        if t < half:
            ring_step(t)

    maybe_ring(1)

    drain(cols.at[pair, core], col_recv)

    def relay(d, _):
        pltpu.make_async_remote_copy(
            src_ref=cols.at[pair, core],
            dst_ref=cols.at[pair, core],
            send_sem=colg_send,
            recv_sem=colg_recv,
            device_id=at(lax.rem(r + 2 * d, n), z),
            device_id_type=MESH,
        ).start()
        return 0

    lax.fori_loop(1, half, relay, 0)

    drain(full.at[pl.ds(0, n - 1)], ag_recv)
    line = lax.broadcasted_iota(jnp.int32, (128, 128), 0)
    across = lax.broadcasted_iota(jnp.int32, (128, 128), 1)
    unit = (lax.rem(line, BW) == lax.rem(across, BW)).astype(F32)
    fisher = full[...].reshape(128, 128) * (1.0 / (n * 256)) + 0.1 * unit

    def split(array):
        array = array.reshape(2, 8, 8, 128)
        return jnp.stack([array[:, i] for i in range(8)], axis=0)

    def block_step(b, carry):
        blocks, inverse = eliminate(*carry, b)
        blocks = pltpu.roll(blocks.reshape(128, 128), 120, 1).reshape(8, 2, 8, 128)
        return rotate(blocks), rotate(inverse)

    maybe_ring(2)
    carry = lax.fori_loop(0, 4, block_step, (split(fisher), split(unit)))
    maybe_ring(3)
    _, inverse = lax.fori_loop(4, 8, block_step, carry)
    whole = jnp.concatenate([inverse[i, m] for m in range(2) for i in range(8)], axis=0)
    linv[...] = whole.reshape(n, depth, 128)

    inv[pair, core, z] = linv[r]

    def spread(d, _):
        pltpu.make_async_remote_copy(
            src_ref=linv.at[r],
            dst_ref=inv.at[pair, core, z],
            send_sem=ze_send,
            recv_sem=ze_recv,
            device_id=at(r, lax.rem(z + d, n)),
            device_id_type=MESH,
        ).start()
        return 0

    lax.fori_loop(1, n, spread, 0)

    other = at(r + 1 - 2 * core, z)

    def swap(buffer, send_sem, recv_sem):
        pltpu.make_async_remote_copy(
            src_ref=buffer.at[:, core],
            dst_ref=buffer.at[:, core],
            send_sem=send_sem,
            recv_sem=recv_sem,
            device_id=other,
            device_id_type=MESH,
        ).start()

    if half > 1:
        drain(cols.at[pl.ds(0, half - 1), 0], colg_recv)
    swap(cols, colx_send, colx_recv)
    maybe_ring(4)

    drain(inv.at[0, 0, pl.ds(0, n - 1)], ze_recv)

    def deal(d, _):
        pltpu.make_async_remote_copy(
            src_ref=inv.at[pair, core],
            dst_ref=inv.at[pair, core],
            send_sem=ig_send,
            recv_sem=ig_recv,
            device_id=at(lax.rem(r + 2 * d, n), z),
            device_id_type=MESH,
        ).start()
        return 0

    lax.fori_loop(1, half, deal, 0)
    maybe_ring(5)
    if half > 1:
        drain(inv.at[pl.ds(0, half - 1), 0], ig_recv)
    swap(inv, ix_send, ix_recv)
    maybe_ring(6)
    maybe_ring(7)
    drain(cols.at[:, 0], colx_recv)
    drain(inv.at[:, 0], ix_recv)
    far = lax.rem(z + half, n)
    arrived(far, 0)
    arrived(far, 1)

    part[...] = jnp.zeros_like(part)

    def plane_step(k, _):
        lower = inv[:, :, k].reshape(2, BW, 128)
        left_side = rows[k].reshape(256, 256)
        right_side = cols[k // 2, lax.rem(k, 2)].reshape(256, 256)
        for m in range(2):
            zero = jnp.zeros((BW, 128), F32)
            matrix = jnp.concatenate(
                [jnp.where(lane < BW, lower[m], zero), jnp.where(lane < BW, zero, lower[m])], axis=0
            )
            high = matrix.astype(BF16)
            rest = (matrix - high.astype(F32)).astype(BF16)

            def whiten(values):
                values = values[:, 128 * m : 128 * m + 128]
                return (
                    lax.dot_general(values, high, NT, preferred_element_type=F32)
                    + lax.dot_general(values, rest, NT, preferred_element_type=F32)
                ).astype(BF16)

            product = lax.dot_general(
                whiten(left_side), whiten(right_side), NT, preferred_element_type=F32
            )
            part[0] += product[:, :128]
            part[1] += product[:, 128:]
        return 0

    lax.fori_loop(0, n, plane_step, 0)

    give = pltpu.make_async_remote_copy(
        src_ref=part.at[1 - x_lo],
        dst_ref=precv,
        send_sem=p_send,
        recv_sem=p_recv,
        device_id={"row": r, "col": (1 - x_lo) * n + z},
        device_id_type=MESH,
    )
    give.start()

    drain(rows.at[pl.ds(0, n - 1)], ring_send)
    for h in range(2):
        target = 2 * lax.rem(r, half) + h

        @pl.when((target != z) | (r != z))
        def _(h=h):
            drain(rows.at[0, 0], col_send.at[h])

    drain(fsend.at[pl.ds(0, n - 1)], rs_send)
    drain(full.at[pl.ds(0, n - 1)], ag_send)
    drain(linv.at[pl.ds(0, n - 1)], ze_send)
    if half > 1:
        drain(cols.at[pl.ds(0, half - 1), 0], colg_send)
        drain(inv.at[pl.ds(0, half - 1), 0], ig_send)
    drain(cols.at[:, 0], colx_send)
    drain(inv.at[:, 0], ix_send)
    give.wait()
    out_ref[...] = (part[x_lo] + precv[...]) * (n * 512) ** (-0.5)


def solution(mesh):
    n = mesh.shape["row"]
    half = n // 2
    depth = 128 // n

    def per_device(grads):
        dma = pltpu.SemaphoreType.DMA
        return pl.pallas_call(
            functools.partial(kernel, n),
            out_shape=jax.ShapeDtypeStruct((256, 128), F32),
            in_specs=[pl.BlockSpec(memory_space=pltpu.VMEM)],
            out_specs=pl.BlockSpec(memory_space=pltpu.VMEM),
            scratch_shapes=[
                pltpu.VMEM((n, 2, 128, 256), BF16),
                pltpu.VMEM((half, 2, 2, 128, 256), BF16),
                pltpu.VMEM((n, depth, 128), F32),
                pltpu.VMEM((n, depth, 128), F32),
                pltpu.VMEM((n, depth, 128), F32),
                pltpu.VMEM((n, depth, 128), F32),
                pltpu.VMEM((half, 2, n, depth, 128), F32),
                pltpu.VMEM((2, 256, 128), F32),
                pltpu.VMEM((256, 128), F32),
                dma,
                dma((n, 2)),
                dma((2,)),
            ]
            + [dma] * 17,
            compiler_params=pltpu.CompilerParams(
                collective_id=0, has_side_effects=True, vmem_limit_bytes=40 * 2**20
            ),
        )(grads)

    return jax.shard_map(
        per_device,
        mesh=mesh,
        in_specs=(P("row", "col"),),
        out_specs=P("row", "col"),
        check_vma=False,
    )
```

time: 523 us -> 87.6 us (0.17)
  waiting for transfers between devices: 449 us -> 0 us
  Pallas kernels: 0 us -> 85 us
  other arithmetic: 49.2 us -> 0 us
  between operations: 13.2 us -> 0.01 us
  matrix products: 7.15 us -> 0 us
    psum x2 -> x0, waiting for transfers between devices: 327 us -> none  [the longest x1 170 us: spread(): return lax.psum(block, axis)]
    all_gather x1 -> x0, waiting for transfers between devices: 122 us -> none  [per_device(): lax.all_gather(whiten(grads, factor(total, total_count)), 'col', axis=1,...]
    pallas_call x0 -> x1, Pallas kernels: none -> 85 us  [per_device(): pl.pallas_call(functools.partial(kernel, n), out_shape=jax.ShapeDtypeStru...]
    another operation x7 -> x0, other arithmetic: 43.4 us -> none  [the longest x4 23.6 us: factor(): lower = jnp.linalg.cholesky(fisher)]
    dot_general x5 -> x0, matrix products: 6.74 us -> none  [the longest x2 5.49 us: product(): lax.dot_general(left, partner, (((1,), (1,)), ((), ())), preferred_elemen...]
  transfers between devices with their start and end apart: 3 -> 0, of which waited for: 3 -> 0; matrix products, arithmetic and copies ran while one was open for 0% -> 0% of each run, Pallas kernels for 0% -> 0%
where the time goes in v1:
time: 87.6 us; the launch traced here: 86.6 us
  Pallas kernels  85 us (97%)
  local copies, waits for them, and re-layouts  1.56 us (2%)
    pallas_call x1, Pallas kernels, per_device(): pl.pallas_call(functools.partial(kernel, n), out_shape=jax.ShapeDtypeStru...  85 us

profile of v1, /device:TPU:1, one launch (start us, length us, event | category | flops | bytes accessed | tf_op | source)
XLA Modules:
  0.0 86.6 jit_solution(12120799861033830543)
XLA Ops:
  0.0 0.0 copy-start
  0.0 0.9 %copy-done = bf16[256,256]{1,0:T(8,128)(2,1)S(1)} copy-done((bf16[256,256]{1,0:T(8,128)(2,1)S(1)}, bf16[256,256]{1,0:T(8,128)(2,1)}, u32[]{:S(2)}) %copy-start) | copy-done | bytes 131096
  0.9 85.0 %shard_map.17 = f32[256,128]{1,0:T(8,128)S(1)} custom-call(bf16[256,256]{1,0:T(8,128)(2,1)S(1)} %copy-done), custom_call_target="tpu_custom_call" | custom-call | tf_op jit(solution)/shard_map/pallas_call | solution.py:394
  85.9 0.7 copy.3
Async XLA Ops:
  0.0 0.9 %copy-start = (bf16[256,256]{1,0:T(8,128)(2,1)S(1)}, bf16[256,256]{1,0:T(8,128)(2,1)}, u32[]{:S(2)}) copy-start(bf16[256,256]{1,0:T(8,128)(2,1)} %g_ref.1) | copy-start | bytes 393220

commit v2 on v1

v2 whole, which is shorter than its diff:
```python
import functools

import jax
import jax.numpy as jnp
from jax import lax
from jax.experimental import pallas as pl
from jax.experimental.pallas import tpu as pltpu
from jax.sharding import PartitionSpec as P

BW = 64
F32 = jnp.float32
BF16 = jnp.bfloat16
MESH = pl.DeviceIdType.MESH
NT = (((1,), (1,)), ((), ()))
TN = (((0,), (0,)), ((), ()))


def eliminate(blocks, inverse):
    lane = lax.broadcasted_iota(jnp.int32, (1, 1, 8, 128), 3)
    sub = lax.broadcasted_iota(jnp.int32, (1, 1, 8, 128), 2)
    low = lane < BW
    for j in range(8):
        row = blocks[0:1, :, j : j + 1, :]
        other = inverse[0:1, :, j : j + 1, :]
        column = jnp.where(low, blocks[:, :, :, j : j + 1], blocks[:, :, :, BW + j : BW + j + 1])
        pivot = column[0:1, :, j : j + 1, :]
        first = jnp.where(sub > j, column[0:1], 0.0)
        column = jnp.concatenate([first, column[1:]], axis=0)
        inverted = 1.0 / pivot
        blocks = blocks - column * (row * inverted)
        inverse = inverse - column * (other * inverted)
        done = jnp.where(sub == j, inverse[0:1] * lax.rsqrt(pivot), inverse[0:1])
        inverse = jnp.concatenate([done, inverse[1:]], axis=0)
    return blocks, inverse


def kernel(
    n,
    g_ref,
    out_ref,
    rows,
    cols,
    fsend,
    frecv,
    full,
    linv,
    inv,
    part,
    precv,
    pre,
    wrow,
    wcol,
    ring_recv,
    col_send,
    p_send,
    p_recv,
    ring_send,
    pre_send,
    pre_recv,
    col_recv,
    colg_send,
    colg_recv,
    colx_send,
    colx_recv,
    rs_send,
    rs_recv,
    ag_send,
    ag_recv,
    ze_send,
    ze_recv,
    ig_send,
    ig_recv,
    ix_send,
    ix_recv,
):
    r = lax.axis_index("row")
    c = lax.axis_index("col")
    half = n // 2
    quad = half // 2
    x_lo = c // n
    z = lax.rem(c, n)
    x_hi = r // half
    q = lax.rem(r, half)
    y = q // 2
    pair = r // 2
    core = lax.rem(r, 2)
    depth = 128 // n

    def at(row, plane):
        return {"row": row, "col": x_lo * n + plane}

    across = {"row": r, "col": (1 - x_lo) * n + z}

    barrier = pltpu.get_barrier_semaphore()

    def greet(d, _):
        pl.semaphore_signal(barrier, 1, device_id=at(lax.rem(r + d, n), z), device_id_type=MESH)
        pl.semaphore_signal(barrier, 1, device_id=at(r, lax.rem(z + d, n)), device_id_type=MESH)
        return 0

    lax.fori_loop(1, n, greet, 0)
    pl.semaphore_signal(barrier, 1, device_id=across, device_id_type=MESH)
    pl.semaphore_wait(barrier, 2 * (n - 1) + 1)

    def push(source, target, send_sem, recv_sem, device):
        copy = pltpu.make_async_remote_copy(
            src_ref=source,
            dst_ref=target,
            send_sem=send_sem,
            recv_sem=recv_sem,
            device_id=device,
            device_id_type=MESH,
        )
        copy.start()
        return copy

    def drain(ref, sem):
        pltpu.make_async_copy(ref, ref, sem).wait()

    def keep_or_push(local, source, target, send_sem, recv_sem, device):
        @pl.when(local)
        def _():
            pltpu.make_async_copy(source, target, recv_sem).start()

        @pl.when(jnp.logical_not(local))
        def _():
            push(source, target, send_sem, recv_sem, device)

    right = lax.rem(z + 1, n)
    left = lax.rem(z + n - 1, n)

    def arrived(slot, chunk):
        drain(rows.at[slot, chunk], ring_recv.at[slot, chunk])

    def ring_step(t):
        if t >= half:
            return
        back = lax.rem(z - t + n, n)
        ahead = lax.rem(z + t, n)
        for slot, chunk, plane, last in (
            (back, 0, right, True),
            (ahead, 1, left, True),
            (back, 1, right, False),
            (ahead, 0, left, False),
        ):
            source = rows.at[slot, chunk]
            if t == 0:
                source = g_ref.at[pl.ds(chunk * 128, 128)]
            else:
                arrived(slot, chunk)
            if t < half - 1 or last:
                push(source, rows.at[slot, chunk], ring_send, ring_recv.at[slot, chunk], at(r, plane))

    ring_step(0)

    gram = lax.dot_general(g_ref[...], g_ref[...], TN, preferred_element_type=F32)
    lane = lax.broadcasted_iota(jnp.int32, (BW, 128), 1)
    packed = jnp.concatenate(
        [
            jnp.where(
                lane < BW,
                gram[128 * m : 128 * m + BW, 128 * m : 128 * m + 128],
                gram[128 * m + BW : 128 * m + 128, 128 * m : 128 * m + 128],
            )
            for m in range(2)
        ],
        axis=0,
    )
    fsend[...] = packed.reshape(n, depth, 128)

    def scatter(d, _):
        to = lax.rem(r + d, n)
        push(fsend.at[to], frecv.at[r], rs_send, rs_recv, at(to, z))
        return 0

    lax.fori_loop(1, n, scatter, 0)

    first = lax.rem(q - z // 2 + half, half)
    hop = x_hi * half + lax.rem(first, quad) * 2 + first // quad
    keep_or_push(hop == r, g_ref, pre, pre_send, pre_recv, at(hop, z))

    frecv[r] = fsend[r]
    rows[z] = g_ref[...].reshape(2, 128, 256)

    drain(frecv.at[pl.ds(0, n - 1)], rs_recv)
    total = frecv[0]
    for i in range(1, n):
        total = total + frecv[i]
    full[r] = total

    def share(d, _):
        push(full.at[r], full.at[r], ag_send, ag_recv, at(lax.rem(r + d, n), z))
        return 0

    lax.fori_loop(1, n, share, 0)

    drain(pre, pre_recv)
    here = 2 * lax.rem(core * quad + y + z // 2, half)
    spot = cols.at[x_hi, core, y]
    for h in range(2):
        keep_or_push(
            here + h == z,
            pre.at[pl.ds(128 * h, 128)],
            spot.at[lax.rem(z, 2)],
            col_send.at[h],
            col_recv,
            at(r, here + h),
        )

    ring_step(1)

    drain(full.at[pl.ds(0, n - 1)], ag_recv)
    line = lax.broadcasted_iota(jnp.int32, (128, 128), 0)
    place = lax.broadcasted_iota(jnp.int32, (128, 128), 1)
    unit = (lax.rem(line, BW) == lax.rem(place, BW)).astype(F32)
    fisher = full[...].reshape(128, 128) * (1.0 / (n * 256)) + 0.1 * unit

    def split(array):
        array = array.reshape(2, 8, 8, 128)
        return jnp.stack([array[:, i] for i in range(8)], axis=0)

    def block_step(b, carry):
        blocks, inverse = eliminate(*carry)
        blocks = pltpu.roll(blocks.reshape(128, 128), 120, 1).reshape(8, 2, 8, 128)
        return (
            jnp.concatenate([blocks[1:], jnp.zeros_like(blocks[:1])], axis=0),
            jnp.concatenate([inverse[1:], inverse[:1]], axis=0),
        )

    ring_step(2)
    carry = lax.fori_loop(0, 5, block_step, (split(fisher), split(unit)))
    ring_step(3)
    _, inverse = lax.fori_loop(5, 8, block_step, carry)
    whole = jnp.concatenate([inverse[i, m] for m in range(2) for i in range(8)], axis=0)
    linv[...] = whole.reshape(n, depth, 128)

    inv[pair, core, z] = linv[r]

    def spread(d, _):
        push(linv.at[r], inv.at[pair, core, z], ze_send, ze_recv, at(r, lax.rem(z + d, n)))
        return 0

    lax.fori_loop(1, n, spread, 0)

    drain(spot, col_recv)

    def relay(d, _):
        push(spot, spot, colg_send, colg_recv, at(lax.rem(r + 2 * d, n), z))
        return 0

    lax.fori_loop(1, half, relay, 0)
    ring_step(4)

    drain(inv.at[0, 0, pl.ds(0, n - 1)], ze_recv)

    def deal(d, _):
        mine = inv.at[pair, core]
        push(mine, mine, ig_send, ig_recv, at(lax.rem(r + 2 * d, n), z))
        return 0

    lax.fori_loop(1, half, deal, 0)

    other = at(r + 1 - 2 * core, z)
    ring_step(5)
    drain(rows.at[pl.ds(0, half - 1)], colg_recv)
    push(cols.at[:, core], cols.at[:, core], colx_send, colx_recv, other)
    drain(inv.at[pl.ds(0, half - 1), 0], ig_recv)
    push(inv.at[:, core], inv.at[:, core], ix_send, ix_recv, other)
    ring_step(6)
    ring_step(7)
    drain(cols.at[:, 0], colx_recv)
    drain(inv.at[:, 0], ix_recv)

    wide = lax.broadcasted_iota(jnp.int32, (BW, 256), 1)

    def whiten_plane(k):
        lower = inv[:, :, k].reshape(2, BW, 128)
        zero = jnp.zeros((BW, 128), F32)
        both = [
            jnp.concatenate([lower[0], zero], axis=1),
            jnp.concatenate([zero, lower[1]], axis=1),
        ]
        matrix = jnp.concatenate(
            [jnp.where(wide // BW == i, both[i // 2], 0.0) for i in range(4)], axis=0
        )
        high = matrix.astype(BF16)
        rest = (matrix - high.astype(F32)).astype(BF16)
        offset = pl.ds(pl.multiple_of(k * 256, 256), 256)
        slot = lax.rem(z // 2 - k // 2 + half, half)

        def whiten(values):
            return (
                lax.dot_general(values, high, NT, preferred_element_type=F32)
                + lax.dot_general(values, rest, NT, preferred_element_type=F32)
            ).astype(BF16)

        wrow[:, offset] = whiten(rows[k].reshape(256, 256))
        for i in range(2):
            values = cols[i, slot // quad, lax.rem(slot, quad), lax.rem(k, 2)]
            wcol[128 * i : 128 * i + 128, offset] = whiten(values)

    def plane_step(d, _):
        whiten_plane(lax.rem(z + half + 1 + d, n))
        return 0

    lax.fori_loop(0, n - 1, plane_step, 0)
    far = lax.rem(z + half, n)
    arrived(far, 0)
    arrived(far, 1)
    whiten_plane(far)

    gives = []
    for i in range(2):
        product = lax.dot_general(
            wrow[128 * i : 128 * i + 128, :], wcol[...], NT, preferred_element_type=F32
        )
        part[0, i] = product[:, :128]
        part[1, i] = product[:, 128:]
        gives.append(
            push(part.at[1 - x_lo, i], precv.at[i], p_send.at[i], p_recv.at[i], across)
        )

    drain(rows.at[pl.ds(0, n - 1)], ring_send)

    @pl.when(hop != r)
    def _():
        drain(pre, pre_send)

    for h in range(2):

        @pl.when(here + h != z)
        def _(h=h):
            drain(rows.at[0, 0], col_send.at[h])

    drain(fsend.at[pl.ds(0, n - 1)], rs_send)
    drain(full.at[pl.ds(0, n - 1)], ag_send)
    drain(linv.at[pl.ds(0, n - 1)], ze_send)
    drain(rows.at[pl.ds(0, half - 1)], colg_send)
    drain(inv.at[pl.ds(0, half - 1), 0], ig_send)
    drain(cols.at[:, 0], colx_send)
    drain(inv.at[:, 0], ix_send)
    for i in range(2):
        gives[i].wait()
        out_ref[128 * i : 128 * i + 128, :] = (part[x_lo, i] + precv[i]) * (n * 512) ** (-0.5)


def solution(mesh):
    n = mesh.shape["row"]
    half = n // 2
    depth = 128 // n

    def per_device(grads):
        dma = pltpu.SemaphoreType.DMA
        return pl.pallas_call(
            functools.partial(kernel, n),
            out_shape=jax.ShapeDtypeStruct((256, 128), F32),
            in_specs=[pl.BlockSpec(memory_space=pltpu.VMEM)],
            out_specs=pl.BlockSpec(memory_space=pltpu.VMEM),
            scratch_shapes=[
                pltpu.VMEM((n, 2, 128, 256), BF16),
                pltpu.VMEM((2, 2, half // 2, 2, 128, 256), BF16),
                pltpu.VMEM((n, depth, 128), F32),
                pltpu.VMEM((n, depth, 128), F32),
                pltpu.VMEM((n, depth, 128), F32),
                pltpu.VMEM((n, depth, 128), F32),
                pltpu.VMEM((half, 2, n, depth, 128), F32),
                pltpu.VMEM((2, 2, 128, 128), F32),
                pltpu.VMEM((2, 128, 128), F32),
                pltpu.VMEM((256, 256), BF16),
                pltpu.VMEM((256, n * 256), BF16),
                pltpu.VMEM((256, n * 256), BF16),
                dma((n, 2)),
                dma((2,)),
                dma((2,)),
                dma((2,)),
            ]
            + [dma] * 18,
            compiler_params=pltpu.CompilerParams(
                collective_id=0, has_side_effects=True, vmem_limit_bytes=40 * 2**20
            ),
        )(grads)

    return jax.shard_map(
        per_device,
        mesh=mesh,
        in_specs=(P("row", "col"),),
        out_specs=P("row", "col"),
        check_vma=False,
    )
```

time: 87.6 us -> 81.3 us (0.928)
  Pallas kernels: 85 us -> 79.1 us
    pallas_call x1, Pallas kernels: 85 us -> 79.1 us  [per_device(): pl.pallas_call(functools.partial(kernel, n), out_shape=jax.ShapeDtypeStru...]
where the time goes in v2:
time: 81.3 us; the launch traced here: 80.6 us
  Pallas kernels  79.1 us (97%)
  local copies, waits for them, and re-layouts  1.56 us (2%)
    pallas_call x1, Pallas kernels, per_device(): pl.pallas_call(functools.partial(kernel, n), out_shape=jax.ShapeDtypeStru...  79.1 us

profile of v2, /device:TPU:1, one launch (start us, length us, event | category | flops | bytes accessed | tf_op | source)
XLA Modules:
  0.0 80.6 jit_solution(11248251533655832579)
XLA Ops:
  0.0 0.0 copy-start
  0.0 0.9 %copy-done = bf16[256,256]{1,0:T(8,128)(2,1)S(1)} copy-done((bf16[256,256]{1,0:T(8,128)(2,1)S(1)}, bf16[256,256]{1,0:T(8,128)(2,1)}, u32[]{:S(2)}) %copy-start) | copy-done | bytes 131096
  0.9 79.1 %shard_map.17 = f32[256,128]{1,0:T(8,128)S(1)} custom-call(bf16[256,256]{1,0:T(8,128)(2,1)S(1)} %copy-done), custom_call_target="tpu_custom_call" | custom-call | tf_op jit(solution)/shard_map/pallas_call | solution.py:354
  80.0 0.7 copy.3
Async XLA Ops:
  0.0 0.9 %copy-start = (bf16[256,256]{1,0:T(8,128)(2,1)S(1)}, bf16[256,256]{1,0:T(8,128)(2,1)}, u32[]{:S(2)}) copy-start(bf16[256,256]{1,0:T(8,128)(2,1)} %g_ref.1) | copy-start | bytes 393220

commit v3 on v2

v3 whole, which is shorter than its diff:
```python
import functools

import jax
import jax.numpy as jnp
from jax import lax
from jax.experimental import pallas as pl
from jax.experimental.pallas import tpu as pltpu
from jax.sharding import PartitionSpec as P

BW = 64
CHUNKS = 4
SIZE = 256 // CHUNKS
F32 = jnp.float32
BF16 = jnp.bfloat16
MESH = pl.DeviceIdType.MESH
NT = (((1,), (1,)), ((), ()))
TN = (((0,), (0,)), ((), ()))


def eliminate(blocks, inverse):
    lane = lax.broadcasted_iota(jnp.int32, (1, 1, 8, 128), 3)
    sub = lax.broadcasted_iota(jnp.int32, (1, 1, 8, 128), 2)
    low = lane < BW
    for start in (0, 4):
        four = range(start, start + 4)
        columns = [
            jnp.where(low, blocks[:, :, :, j : j + 1], blocks[:, :, :, BW + j : BW + j + 1])
            for j in four
        ]
        factor = [[None] * 4 for _ in range(4)]
        root = [None] * 4
        for v in range(4):
            for u in range(v, 4):
                entry = columns[v][0:1, :, start + u : start + u + 1, :]
                for w in range(v):
                    entry = entry - factor[u][w] * factor[v][w]
                if u == v:
                    root[v] = lax.rsqrt(entry)
                else:
                    factor[u][v] = entry * root[v]

        def solve(array):
            forward = []
            for u in range(4):
                row = array[0:1, :, start + u : start + u + 1, :]
                for w in range(u):
                    row = row - factor[u][w] * forward[w]
                forward.append(row * root[u])
            back = [None] * 4
            for u in reversed(range(4)):
                row = forward[u]
                for w in range(u + 1, 4):
                    row = row - factor[w][u] * back[w]
                back[u] = row * root[u]
            return forward, back

        _, take = solve(blocks)
        done, other = solve(inverse)
        columns = [
            jnp.concatenate([jnp.where(sub > start + 3, column[0:1], 0.0), column[1:]], axis=0)
            for column in columns
        ]
        for v in range(4):
            blocks = blocks - columns[v] * take[v]
            inverse = inverse - columns[v] * other[v]
        top = inverse[0:1]
        for u in range(4):
            top = jnp.where(sub == start + u, done[u], top)
        inverse = jnp.concatenate([top, inverse[1:]], axis=0)
    return blocks, inverse


def kernel(
    n,
    g_ref,
    out_ref,
    rows,
    cols,
    fsend,
    frecv,
    full,
    linv,
    inv,
    part,
    precv,
    pre,
    wrow,
    wcol,
    ring_recv,
    col_send,
    p_send,
    p_recv,
    ring_send,
    pre_send,
    pre_recv,
    col_recv,
    colg_send,
    colg_recv,
    colx_send,
    colx_recv,
    rs_send,
    rs_recv,
    ag_send,
    ag_recv,
    ze_send,
    ze_recv,
    ig_send,
    ig_recv,
    ix_send,
    ix_recv,
):
    r = lax.axis_index("row")
    c = lax.axis_index("col")
    half = n // 2
    quad = half // 2
    x_lo = c // n
    z = lax.rem(c, n)
    x_hi = r // half
    q = lax.rem(r, half)
    y = q // 2
    pair = r // 2
    core = lax.rem(r, 2)
    depth = 128 // n

    def at(row, plane):
        return {"row": row, "col": x_lo * n + plane}

    across = {"row": r, "col": (1 - x_lo) * n + z}

    barrier = pltpu.get_barrier_semaphore()

    def greet(d, _):
        pl.semaphore_signal(barrier, 1, device_id=at(lax.rem(r + d, n), z), device_id_type=MESH)
        pl.semaphore_signal(barrier, 1, device_id=at(r, lax.rem(z + d, n)), device_id_type=MESH)
        return 0

    lax.fori_loop(1, n, greet, 0)
    pl.semaphore_signal(barrier, 1, device_id=across, device_id_type=MESH)
    pl.semaphore_wait(barrier, 2 * (n - 1) + 1)

    def push(source, target, send_sem, recv_sem, device):
        copy = pltpu.make_async_remote_copy(
            src_ref=source,
            dst_ref=target,
            send_sem=send_sem,
            recv_sem=recv_sem,
            device_id=device,
            device_id_type=MESH,
        )
        copy.start()
        return copy

    def drain(ref, sem):
        pltpu.make_async_copy(ref, ref, sem).wait()

    def keep_or_push(local, source, target, send_sem, recv_sem, device):
        @pl.when(local)
        def _():
            pltpu.make_async_copy(source, target, recv_sem).start()

        @pl.when(jnp.logical_not(local))
        def _():
            push(source, target, send_sem, recv_sem, device)

    right = lax.rem(z + 1, n)
    left = lax.rem(z + n - 1, n)

    def arrived(slot, chunk):
        drain(rows.at[slot, chunk], ring_recv.at[slot, chunk])

    def ring_step(t):
        if t >= half:
            return
        back = lax.rem(z - t + n, n)
        ahead = lax.rem(z + t, n)
        for i in range(CHUNKS):
            for slot, chunk, plane in ((back, i, right), (ahead, CHUNKS - 1 - i, left)):
                source = rows.at[slot, chunk]
                if t == 0:
                    source = g_ref.at[pl.ds(chunk * SIZE, SIZE)]
                else:
                    arrived(slot, chunk)
                if t < half - 1 or i < CHUNKS // 2:
                    push(
                        source,
                        rows.at[slot, chunk],
                        ring_send,
                        ring_recv.at[slot, chunk],
                        at(r, plane),
                    )

    lane = lax.broadcasted_iota(jnp.int32, (BW, 128), 1)
    line = lax.broadcasted_iota(jnp.int32, (128, 128), 0)
    place = lax.broadcasted_iota(jnp.int32, (128, 128), 1)
    unit = (lax.rem(line, BW) == lax.rem(place, BW)).astype(F32)
    other = at(r + 1 - 2 * core, z)

    def fisher_scatter():
        gram = lax.dot_general(g_ref[...], g_ref[...], TN, preferred_element_type=F32)
        packed = jnp.concatenate(
            [
                jnp.where(
                    lane < BW,
                    gram[128 * m : 128 * m + BW, 128 * m : 128 * m + 128],
                    gram[128 * m + BW : 128 * m + 128, 128 * m : 128 * m + 128],
                )
                for m in range(2)
            ],
            axis=0,
        )
        fsend[...] = packed.reshape(n, depth, 128)

        def scatter(d, _):
            to = lax.rem(r + d, n)
            push(fsend.at[to], frecv.at[r], rs_send, rs_recv, at(to, z))
            return 0

        lax.fori_loop(1, n, scatter, 0)
        frecv[r] = fsend[r]

    first = lax.rem(q - z // 2 + half, half)
    hop = x_hi * half + lax.rem(first, quad) * 2 + first // quad

    def columns_hop():
        keep_or_push(hop == r, g_ref, pre, pre_send, pre_recv, at(hop, z))
        rows[z] = g_ref[...].reshape(CHUNKS, SIZE, 256)

    def fisher_share():
        drain(frecv.at[pl.ds(0, n - 1)], rs_recv)
        total = frecv[0]
        for i in range(1, n):
            total = total + frecv[i]
        full[r] = total

        def share(d, _):
            push(full.at[r], full.at[r], ag_send, ag_recv, at(lax.rem(r + d, n), z))
            return 0

        lax.fori_loop(1, n, share, 0)

    here = 2 * lax.rem(core * quad + y + z // 2, half)
    spot = cols.at[x_hi, core, y]

    def columns_along():
        drain(pre, pre_recv)
        for h in range(2):
            keep_or_push(
                here + h == z,
                pre.at[pl.ds(128 * h, 128)],
                spot.at[lax.rem(z, 2)],
                col_send.at[h],
                col_recv,
                at(r, here + h),
            )

    def fisher_matrix():
        drain(full.at[pl.ds(0, n - 1)], ag_recv)
        fisher = full[...].reshape(128, 128) * (1.0 / (n * 256)) + 0.1 * unit
        return split(fisher), split(unit)

    def split(array):
        array = array.reshape(2, 8, 8, 128)
        return jnp.stack([array[:, i] for i in range(8)], axis=0)

    def block_step(b, carry):
        blocks, inverse = eliminate(*carry)
        blocks = pltpu.roll(blocks.reshape(128, 128), 120, 1).reshape(8, 2, 8, 128)
        return (
            jnp.concatenate([blocks[1:], jnp.zeros_like(blocks[:1])], axis=0),
            jnp.concatenate([inverse[1:], inverse[:1]], axis=0),
        )

    def inverse_along(inverse):
        whole = jnp.concatenate([inverse[i, m] for m in range(2) for i in range(8)], axis=0)
        linv[...] = whole.reshape(n, depth, 128)
        inv[pair, core, z] = linv[r]

        def spread(d, _):
            push(linv.at[r], inv.at[pair, core, z], ze_send, ze_recv, at(r, lax.rem(z + d, n)))
            return 0

        lax.fori_loop(1, n, spread, 0)

    def columns_gather():
        drain(spot, col_recv)

        def relay(d, _):
            push(spot, spot, colg_send, colg_recv, at(lax.rem(r + 2 * d, n), z))
            return 0

        lax.fori_loop(1, half, relay, 0)

    def inverse_gather():
        drain(inv.at[0, 0, pl.ds(0, n - 1)], ze_recv)

        def deal(d, _):
            mine = inv.at[pair, core]
            push(mine, mine, ig_send, ig_recv, at(lax.rem(r + 2 * d, n), z))
            return 0

        lax.fori_loop(1, half, deal, 0)

    def columns_swap():
        drain(rows.at[pl.ds(0, half - 1)], colg_recv)
        push(cols.at[:, core], cols.at[:, core], colx_send, colx_recv, other)

    def inverse_swap():
        drain(inv.at[pl.ds(0, half - 1), 0], ig_recv)
        push(inv.at[:, core], inv.at[:, core], ix_send, ix_recv, other)

    columns_hop()
    ring_step(0)
    fisher_scatter()
    columns_along()
    ring_step(1)
    fisher_share()
    carry = fisher_matrix()
    ring_step(2)
    carry = lax.fori_loop(0, 4, block_step, carry)
    columns_gather()
    carry = lax.fori_loop(4, 8, block_step, carry)
    inverse_along(carry[1])
    ring_step(3)
    ring_step(4)
    inverse_gather()
    ring_step(5)
    ring_step(6)
    inverse_swap()
    ring_step(7)
    columns_swap()
    drain(inv.at[:, 0], ix_recv)
    drain(cols.at[:, 0], colx_recv)

    wide = lax.broadcasted_iota(jnp.int32, (BW, 256), 1)

    def whiten_plane(k):
        lower = inv[:, :, k].reshape(2, BW, 128)
        zero = jnp.zeros((BW, 128), F32)
        both = [
            jnp.concatenate([lower[0], zero], axis=1),
            jnp.concatenate([zero, lower[1]], axis=1),
        ]
        matrix = jnp.concatenate(
            [jnp.where(wide // BW == i, both[i // 2], 0.0) for i in range(4)], axis=0
        )
        high = matrix.astype(BF16)
        rest = (matrix - high.astype(F32)).astype(BF16)
        offset = pl.ds(pl.multiple_of(k * 256, 256), 256)
        slot = lax.rem(z // 2 - k // 2 + half, half)

        where = (slot // quad, lax.rem(slot, quad), lax.rem(k, 2))
        values = jnp.concatenate(
            [rows[k].reshape(256, 256), cols[(0, *where)], cols[(1, *where)]], axis=0
        )
        white = lax.dot_general(
            jnp.concatenate([values, values], axis=1),
            jnp.concatenate([high, rest], axis=1),
            NT,
            preferred_element_type=F32,
        ).astype(BF16)
        wrow[:, offset] = white[:256]
        wcol[0, :, offset] = white[256:384]
        wcol[1, :, offset] = white[384:]

    def plane_step(d, _):
        whiten_plane(lax.rem(z + half + 1 + d, n))
        return 0

    lax.fori_loop(0, n - 1, plane_step, 0, unroll=3)
    far = lax.rem(z + half, n)
    for i in range(CHUNKS):
        arrived(far, i)
    whiten_plane(far)

    def product(i):
        return lax.dot_general(wrow[...], wcol[i], NT, preferred_element_type=F32)

    part[...] = product(1 - x_lo)
    give = push(part, precv, p_send, p_recv, across)
    own = product(x_lo)

    drain(rows.at[pl.ds(0, n - 1)], ring_send)

    @pl.when(hop != r)
    def _():
        drain(pre, pre_send)

    for h in range(2):

        @pl.when(here + h != z)
        def _(h=h):
            drain(cols.at[0, 0, 0, 0], col_send.at[h])

    drain(fsend.at[pl.ds(0, n - 1)], rs_send)
    drain(full.at[pl.ds(0, n - 1)], ag_send)
    drain(linv.at[pl.ds(0, n - 1)], ze_send)
    drain(rows.at[pl.ds(0, half - 1)], colg_send)
    drain(inv.at[pl.ds(0, half - 1), 0], ig_send)
    drain(cols.at[:, 0], colx_send)
    drain(inv.at[:, 0], ix_send)
    give.wait()
    out_ref[...] = (own + precv[...]) * (n * 512) ** (-0.5)


def solution(mesh):
    n = mesh.shape["row"]
    half = n // 2
    depth = 128 // n

    def per_device(grads):
        dma = pltpu.SemaphoreType.DMA
        return pl.pallas_call(
            functools.partial(kernel, n),
            out_shape=jax.ShapeDtypeStruct((256, 128), F32),
            in_specs=[pl.BlockSpec(memory_space=pltpu.VMEM)],
            out_specs=pl.BlockSpec(memory_space=pltpu.VMEM),
            scratch_shapes=[
                pltpu.VMEM((n, CHUNKS, SIZE, 256), BF16),
                pltpu.VMEM((2, 2, half // 2, 2, 128, 256), BF16),
                pltpu.VMEM((n, depth, 128), F32),
                pltpu.VMEM((n, depth, 128), F32),
                pltpu.VMEM((n, depth, 128), F32),
                pltpu.VMEM((n, depth, 128), F32),
                pltpu.VMEM((half, 2, n, depth, 128), F32),
                pltpu.VMEM((256, 128), F32),
                pltpu.VMEM((256, 128), F32),
                pltpu.VMEM((256, 256), BF16),
                pltpu.VMEM((256, n * 256), BF16),
                pltpu.VMEM((2, 128, n * 256), BF16),
                dma((n, CHUNKS)),
                dma((2,)),
            ]
            + [dma] * 20,
            compiler_params=pltpu.CompilerParams(
                collective_id=0, has_side_effects=True, vmem_limit_bytes=40 * 2**20
            ),
        )(grads)

    return jax.shard_map(
        per_device,
        mesh=mesh,
        in_specs=(P("row", "col"),),
        out_specs=P("row", "col"),
        check_vma=False,
    )
```

time: 81.3 us -> 69.7 us (0.86)
  Pallas kernels: 79.1 us -> 68 us
    pallas_call x1, Pallas kernels: 79.1 us -> 68 us  [per_device(): pl.pallas_call(functools.partial(kernel, n), out_shape=jax.ShapeDtypeStru...]
where the time goes in v3:
time: 69.7 us; the launch traced here: 69.5 us
  Pallas kernels  68 us (98%)
  local copies, waits for them, and re-layouts  1.56 us (2%)
    pallas_call x1, Pallas kernels, per_device(): pl.pallas_call(functools.partial(kernel, n), out_shape=jax.ShapeDtypeStru...  68 us
    unnamed x3, local copies, waits for them, and re-layouts  1.56 us

profile of v3, /device:TPU:1, one launch (start us, length us, event | category | flops | bytes accessed | tf_op | source)
XLA Modules:
  0.0 69.5 jit_solution(3615486975763477873)
XLA Ops:
  0.0 0.0 copy-start
  0.0 0.9 %copy-done = bf16[256,256]{1,0:T(8,128)(2,1)S(1)} copy-done((bf16[256,256]{1,0:T(8,128)(2,1)S(1)}, bf16[256,256]{1,0:T(8,128)(2,1)}, u32[]{:S(2)}) %copy-start) | copy-done | bytes 131096
  0.9 68.0 %shard_map.17 = f32[256,128]{1,0:T(8,128)S(1)} custom-call(bf16[256,256]{1,0:T(8,128)(2,1)S(1)} %copy-done), custom_call_target="tpu_custom_call" | custom-call | tf_op jit(solution)/shard_map/pallas_call | solution.py:412
  68.9 0.7 copy.3
Async XLA Ops:
  0.0 0.9 %copy-start = (bf16[256,256]{1,0:T(8,128)(2,1)S(1)}, bf16[256,256]{1,0:T(8,128)(2,1)}, u32[]{:S(2)}) copy-start(bf16[256,256]{1,0:T(8,128)(2,1)} %g_ref.1) | copy-start | bytes 393220

commit v4 on v3

--- a/solution.py
+++ b/solution.py
@@ -218,8 +218,14 @@
         lax.fori_loop(1, n, scatter, 0)
         frecv[r] = fsend[r]
 
-    first = lax.rem(q - z // 2 + half, half)
-    hop = x_hi * half + lax.rem(first, quad) * 2 + first // quad
+    def spot_of(m):
+        if quad == 1:
+            return m, 0
+        return lax.rem(m // 2, 2), m // 4 * 2 + lax.rem(m, 2)
+
+    hop_core, hop_y = spot_of(lax.rem(q + 3 * (z // 2), half))
+    hop = x_hi * half + hop_y * 2 + hop_core
+    me = core if quad == 1 else y // 2 * 4 + core * 2 + lax.rem(y, 2)
 
     def columns_hop():
         keep_or_push(hop == r, g_ref, pre, pre_send, pre_recv, at(hop, z))
@@ -238,7 +244,7 @@
 
         lax.fori_loop(1, n, share, 0)
 
-    here = 2 * lax.rem(core * quad + y + z // 2, half)
+    here = 2 * lax.rem(me + (4 * half - 3) * (z // 2), half)
     spot = cols.at[x_hi, core, y]
 
     def columns_along():
@@ -308,18 +314,17 @@
         drain(inv.at[pl.ds(0, half - 1), 0], ig_recv)
         push(inv.at[:, core], inv.at[:, core], ix_send, ix_recv, other)
 
-    columns_hop()
     ring_step(0)
     fisher_scatter()
+    columns_hop()
+    fisher_share()
+    ring_step(1)
     columns_along()
-    ring_step(1)
-    fisher_share()
     carry = fisher_matrix()
     ring_step(2)
-    carry = lax.fori_loop(0, 4, block_step, carry)
+    carry = lax.fori_loop(0, 8, block_step, carry)
+    inverse_along(carry[1])
     columns_gather()
-    carry = lax.fori_loop(4, 8, block_step, carry)
-    inverse_along(carry[1])
     ring_step(3)
     ring_step(4)
     inverse_gather()
@@ -346,9 +351,9 @@
         high = matrix.astype(BF16)
         rest = (matrix - high.astype(F32)).astype(BF16)
         offset = pl.ds(pl.multiple_of(k * 256, 256), 256)
-        slot = lax.rem(z // 2 - k // 2 + half, half)
-
-        where = (slot // quad, lax.rem(slot, quad), lax.rem(k, 2))
+        slot = spot_of(lax.rem(z // 2 + 3 * (k // 2), half))
+
+        where = (*slot, lax.rem(k, 2))
         values = jnp.concatenate(
             [rows[k].reshape(256, 256), cols[(0, *where)], cols[(1, *where)]], axis=0
         )

time: 69.7 us -> 68.5 us (0.983)
  Pallas kernels: 68 us -> 66.4 us
    pallas_call x1, Pallas kernels: 68 us -> 66.4 us  [per_device(): pl.pallas_call(functools.partial(kernel, n), out_shape=jax.ShapeDtypeStru...]
where the time goes in v4:
time: 68.5 us; the launch traced here: 67.9 us
  Pallas kernels  66.4 us (97%)
  local copies, waits for them, and re-layouts  1.56 us (2%)
    pallas_call x1, Pallas kernels, per_device(): pl.pallas_call(functools.partial(kernel, n), out_shape=jax.ShapeDtypeStru...  66.4 us
    unnamed x3, local copies, waits for them, and re-layouts  1.56 us

profile of v4, /device:TPU:1, one launch (start us, length us, event | category | flops | bytes accessed | tf_op | source)
XLA Modules:
  0.0 67.9 jit_solution(5650656086569718469)
XLA Ops:
  0.0 0.0 copy-start
  0.0 0.9 %copy-done = bf16[256,256]{1,0:T(8,128)(2,1)S(1)} copy-done((bf16[256,256]{1,0:T(8,128)(2,1)S(1)}, bf16[256,256]{1,0:T(8,128)(2,1)}, u32[]{:S(2)}) %copy-start) | copy-done | bytes 131096
  0.9 66.4 %shard_map.17 = f32[256,128]{1,0:T(8,128)S(1)} custom-call(bf16[256,256]{1,0:T(8,128)(2,1)S(1)} %copy-done), custom_call_target="tpu_custom_call" | custom-call | tf_op jit(solution)/shard_map/pallas_call | solution.py:417
  67.3 0.7 copy.3
Async XLA Ops:
  0.0 0.9 %copy-start = (bf16[256,256]{1,0:T(8,128)(2,1)S(1)}, bf16[256,256]{1,0:T(8,128)(2,1)}, u32[]{:S(2)}) copy-start(bf16[256,256]{1,0:T(8,128)(2,1)} %g_ref.1) | copy-start | bytes 393220

commit v5 on v4

--- a/solution.py
+++ b/solution.py
@@ -322,10 +322,11 @@
     columns_along()
     carry = fisher_matrix()
     ring_step(2)
-    carry = lax.fori_loop(0, 8, block_step, carry)
+    carry = lax.fori_loop(0, 5, block_step, carry)
+    ring_step(3)
+    carry = lax.fori_loop(5, 8, block_step, carry)
     inverse_along(carry[1])
     columns_gather()
-    ring_step(3)
     ring_step(4)
     inverse_gather()
     ring_step(5)

time: 68.5 us -> 74.5 us (1.088)
  Pallas kernels: 66.4 us -> 72 us
    pallas_call x1, Pallas kernels: 66.4 us -> 72 us  [per_device(): pl.pallas_call(functools.partial(kernel, n), out_shape=jax.ShapeDtypeStru...]
where the time goes in v5:
time: 74.5 us; the launch traced here: 73.6 us
  Pallas kernels  72 us (97%)
  local copies, waits for them, and re-layouts  1.56 us (2%)
    pallas_call x1, Pallas kernels, per_device(): pl.pallas_call(functools.partial(kernel, n), out_shape=jax.ShapeDtypeStru...  72 us
    unnamed x3, local copies, waits for them, and re-layouts  1.56 us

profile of v5, /device:TPU:1, one launch (start us, length us, event | category | flops | bytes accessed | tf_op | source)
XLA Modules:
  0.0 73.6 jit_solution(6329941616448853225)
XLA Ops:
  0.0 0.0 copy-start
  0.0 0.9 %copy-done = bf16[256,256]{1,0:T(8,128)(2,1)S(1)} copy-done((bf16[256,256]{1,0:T(8,128)(2,1)S(1)}, bf16[256,256]{1,0:T(8,128)(2,1)}, u32[]{:S(2)}) %copy-start) | copy-done | bytes 131096
  0.9 72.0 %shard_map.17 = f32[256,128]{1,0:T(8,128)S(1)} custom-call(bf16[256,256]{1,0:T(8,128)(2,1)S(1)} %copy-done), custom_call_target="tpu_custom_call" | custom-call | tf_op jit(solution)/shard_map/pallas_call | solution.py:418
  72.9 0.7 copy.3
Async XLA Ops:
  0.0 0.9 %copy-start = (bf16[256,256]{1,0:T(8,128)(2,1)S(1)}, bf16[256,256]{1,0:T(8,128)(2,1)}, u32[]{:S(2)}) copy-start(bf16[256,256]{1,0:T(8,128)(2,1)} %g_ref.1) | copy-start | bytes 393220
